TPU v7x, 256 devices: a whole 4x4x8 slice. The times are simulated.
256 devices in a mesh: dp: 32 (over x, y, core), vocab: 8 (over z).
Axes of the slice: x: 4, y: 4, z: 8, core: 2. Of those that a mesh axis runs over, the one named last changes fastest.
Arguments:
- student_hidden: bfloat16 [768, 3584], P('dp'), may hold values from -110 to 110
- teacher_hidden: bfloat16 [768, 4608], P('dp'), may hold values from -110 to 110
- student_head: bfloat16 [3584, 131072], P(None, ('dp', 'vocab')), may hold values from -0.09375 to 0.09375
- teacher_head: bfloat16 [4608, 131072], P(None, ('dp', 'vocab')), may hold values from -0.09375 to 0.09375
- live_count: int32 [32], P('dp'), may hold values from 1 to 24, as said below
- teacher_count: int32 [32], P('dp'), may hold values from 1 to 24, as said below
- teacher_dest: int32 [768], P('dp'), may hold values from 0 to 767, as said below
Outputs:
- distill_loss: float32 [], replicated
- grad_hidden: bfloat16 [768, 3584], P('dp', 'vocab')
- grad_head: bfloat16 [3584, 131072], P(None, ('dp', 'vocab'))
Inputs may be any that keep to these rules, and one draw needn't show every extreme that they name: Shard s's covered tokens are its first live_count[s] tokens; the counts sum to 384. Data shard j's filled teacher row slots are its first teacher_count[j] slots; the counts sum to 384. `teacher_dest`: A filled slot names the global index of a covered token; every covered token is named by exactly one filled slot. Unfilled slots hold arbitrary indices.
All inputs are finite; a program needn't handle non-finite values.
Results may differ from a plain program's by a relative error of at most 0.014.
Values may be sent and summed in bfloat16 or wider, within the bound.
No kernel may reach another device: no remote copies, remote signals or barrier semaphores. Data moves between devices by JAX's collectives and lax.ppermute only.
A program may use at most 128 MiB of HBM per device.

v0:
```python
import jax
import jax.numpy as jnp
from jax import lax
from jax.sharding import PartitionSpec as P

loss_scale = 65536.0


def per_device(
    student_hidden,
    teacher_hidden,
    student_head,
    teacher_head,
    live_count,
    teacher_count,
    teacher_dest,
):
    tok_dev = student_hidden.shape[0]
    data_size = lax.axis_size("dp")
    token_count = tok_dev * data_size
    live_total = token_count // 2
    grad_scale = loss_scale / live_total
    live_all, teach_all, dest_all = (
        lax.all_gather(live_count, "dp", axis=0, tiled=True),
        lax.all_gather(teacher_count, "dp", axis=0, tiled=True),
        lax.all_gather(teacher_dest, "dp", axis=0, tiled=True),
    )
    position = lax.broadcasted_iota(jnp.int32, (data_size, tok_dev), 1)
    live_flag = (position < live_all[:, None]).reshape(-1)
    slot_ok = (position < teach_all[:, None]).reshape(-1)
    gathered = lax.all_gather(student_hidden, "dp", axis=0, tiled=True)
    vocab_rows = student_head.shape[1]
    student_logits = jnp.dot(gathered, student_head, preferred_element_type=jnp.float32)
    packed = jnp.dot(
        lax.all_gather(teacher_hidden, "dp", axis=0, tiled=True),
        teacher_head,
        preferred_element_type=jnp.float32,
    )
    target = jnp.where(slot_ok, dest_all, token_count)
    teacher_logits = (
        jnp.zeros((token_count, vocab_rows), jnp.float32).at[target].set(packed, mode="drop")
    )
    teacher_top, student_top = lax.pmax(
        (jnp.max(teacher_logits, axis=1), jnp.max(student_logits, axis=1)), ("dp", "vocab")
    )
    teacher_weights = jnp.exp(teacher_logits - teacher_top[:, None])
    teacher_sum, student_sum, cross_sum = lax.psum(
        (
            jnp.sum(teacher_weights, axis=1),
            jnp.sum(jnp.exp(student_logits - student_top[:, None]), axis=1),
            jnp.sum(teacher_weights * (teacher_logits - student_logits), axis=1),
        ),
        ("dp", "vocab"),
    )
    teacher_norm = teacher_top + jnp.log(teacher_sum)
    student_norm = student_top + jnp.log(student_sum)
    divergence = cross_sum / teacher_sum - teacher_norm + student_norm
    distill_loss = jnp.sum(jnp.where(live_flag, divergence, 0.0)) / live_total
    probs_gap = jnp.exp(student_logits - student_norm[:, None]) - jnp.exp(
        teacher_logits - teacher_norm[:, None]
    )
    logit_grad = jnp.where(live_flag[:, None], probs_gap * grad_scale, 0.0).astype(jnp.bfloat16)
    grad_head = lax.dot_general(
        gathered, logit_grad, (((0,), (0,)), ((), ())), preferred_element_type=jnp.float32
    ).astype(jnp.bfloat16)
    columns = student_head.shape[0] // lax.axis_size("vocab")
    summed = lax.psum(
        lax.dot_general(
            logit_grad, student_head, (((1,), (1,)), ((), ())), preferred_element_type=jnp.float32
        ),
        ("dp", "vocab"),
    )
    own_block = lax.dynamic_slice(
        summed,
        (lax.axis_index("dp") * tok_dev, lax.axis_index("vocab") * columns),
        (tok_dev, columns),
    )
    return (distill_loss, own_block.astype(jnp.bfloat16), grad_head)


def solution(mesh):
    return jax.shard_map(
        per_device,
        mesh=mesh,
        in_specs=(
            P("dp", None),
            P("dp", None),
            P(None, ("dp", "vocab")),
            P(None, ("dp", "vocab")),
            P("dp"),
            P("dp"),
            P("dp"),
        ),
        out_specs=(P(), P("dp", "vocab"), P(None, ("dp", "vocab"))),
        check_vma=False,
    )
```

profile of v0, /device:TPU:1, one launch (start us, length us, event | category | flops | bytes accessed | tf_op | source)
XLA Modules:
  0.0 473.6 jit_solution(16044244641711408158)
XLA Ops:
  7.2 0.0 all-gather.5.cloned.1.call-start
  7.2 0.7 all-gather.5.cloned.1.call-update
  7.9 0.0 all-gather.3.cloned.1.call-start
  7.9 0.7 all-gather.3.cloned.1.call-update
  9.9 1.3 dynamic-slice
  11.9 0.8 dynamic-update-slice
  12.6 0.8 dynamic-update-slice.1
  13.4 0.8 dynamic-update-slice.2
  14.2 14.7 %all-reduce.3 = (s32[32]{0:T(128)S(1)}, s32[32]{0:T(128)S(1)}, s32[768]{0:T(1024)S(1)}) all-reduce(s32[32]{0:T(128)S(1)} %dynamic-update-slice, s32[32]{0:T(128)S(1)} %dynamic-update-slice.1, s32[768]{0:T(1024)S(1)} %dynamic-update-slice.2), channel_id=1, replica_groups=mesh['dp'=32,'vocab'=8] {'dp'}, use_global_device_ids=true, to_apply=%add | all-reduce | flops 832 | bytes 6656
  28.9 0.1 iota_compare_fusion.1
  29.0 0.1 lt.42
  29.1 0.1 iota_compare_fusion
  29.2 0.1 lt.45
  29.3 38.4 %all-gather.5.cloned.1.call-done = bf16[768,3584]{1,0:T(8,128)(2,1)} async-done(((bf16[24,3584]{1,0:T(8,128)(2,1)}), bf16[768,3584]{1,0:T(8,128)(2,1)}) %all-gather.5.cloned.1.call-update) | async-done | bytes 5505040 | tf_op jit(solution)/shard_map/all_gather | solution.py:31
  67.7 7.9 %fusion.4 = (f32[768]{0:T(1024)S(1)}, f32[768,512]{0,1:T(8,128)}) fusion(bf16[768,3584]{1,0:T(8,128)(2,1)} %all-gather.5.cloned.1.call-done, bf16[3584,512]{1,0:T(8,128)(2,1)} %param.9), kind=kOutput, calls=%fused_computation.17 | convolution fusion | flops 2818964736 | bytes 10750976 | tf_op jit(solution)/shard_map/dot_general | solution.py:33
  75.6 49.5 %all-gather.3.cloned.1.call-done = bf16[768,4608]{1,0:T(8,128)(2,1)} async-done(((bf16[24,4608]{1,0:T(8,128)(2,1)}), bf16[768,4608]{1,0:T(8,128)(2,1)}) %all-gather.3.cloned.1.call-update) | async-done | bytes 7077904 | tf_op jit(solution)/shard_map/all_gather | solution.py:35
  125.1 9.3 %fusion.5 = f32[768,512]{1,0:T(8,128)} fusion(bf16[768,4608]{1,0:T(8,128)(2,1)} %all-gather.3.cloned.1.call-done, bf16[4608,512]{1,0:T(8,128)(2,1)} %param.10), kind=kOutput, calls=%fused_computation.18 | convolution fusion | flops 3623878656 | bytes 13369344 | tf_op jit(solution)/shard_map/dot_general | solution.py:34
  134.4 6.6 %scatter_custom_fusion = f32[768,512]{1,0:T(8,128)S(1)} fusion(s32[768]{0:T(1024)S(1)} %compare_select_fusion, f32[768,512]{1,0:T(8,128)} %fusion.5, f32[]{:T(128)} %constant.12.clone.1), kind=kCustom, calls=%fused_computation.8 | custom fusion | bytes 1573376 | tf_op jit(solution)/shard_map/scatter | solution.py:41
  141.0 0.5 copy.12
  141.5 0.2 reduce_max.18
  141.6 75.6 %all-reduce.6 = (f32[768]{0:T(1024)S(1)}, f32[768]{0:T(1024)S(1)}) all-reduce(f32[768]{0:T(1024)S(1)} %get-tuple-element.21, f32[768]{0:T(1024)S(1)} %reduce_max.18), channel_id=1, replica_groups=mesh['dp'=32,'vocab'=8] {'dp','vocab'}, use_global_device_ids=true, to_apply=%region_8.9 | all-reduce | flops 1536 | bytes 12288 | tf_op jit(solution)/shard_map/pmax | solution.py:43
  217.3 0.0 copy-start
  217.3 2.1 multiply_reduce_fusion
  219.4 74.5 %all-reduce.5 = (f32[768]{0:T(1024)S(1)}, f32[768]{0:T(1024)S(1)}) all-reduce(f32[768]{0:T(1024)S(1)} %get-tuple-element.11, f32[768]{0:T(1024)S(1)} %get-tuple-element.10), channel_id=1, replica_groups=mesh['dp'=32,'vocab'=8] {'dp','vocab'}, use_global_device_ids=true, to_apply=%region_10.11 | all-reduce | flops 1536 | bytes 12288 | tf_op jit(solution)/shard_map/psum | solution.py:47
  293.9 0.0 copy-done
  293.9 0.0 slice-start
  293.9 0.5 select_convert_fusion
  294.4 0.0 slice-start.1
  294.4 8.2 %fusion.6 = f32[768,3584]{1,0:T(8,128)} fusion(bf16[768,512]{0,1:T(8,128)(2,1)S(1)} %select_convert_fusion, bf16[3584,512]{1,0:T(8,128)(2,1)} %param.9), kind=kOutput, calls=%fused_computation.19 | convolution fusion | flops 2818572288 | bytes 15466496 | tf_op jit(solution)/shard_map/dot_general | solution.py:68
  302.6 0.0 slice-done
  302.6 0.0 slice-done.1
  302.6 4.5 fusion
  307.1 5.9 %copy.15 = bf16[3584,512]{1,0:T(8,128)(2,1)} copy(bf16[3584,512]{0,1:T(8,128)(2,1)} %fusion) | data formatting | bytes 7340032
  313.0 149.9 %all-reduce.8 = (f32[768]{0:T(1024)S(1)}, bf16[768,3584]{1,0:T(8,128)(2,1)}) all-reduce(f32[768]{0:T(1024)S(1)} %get-tuple-element.9, f32[768,3584]{1,0:T(8,128)} %fusion.6), channel_id=1, replica_groups=mesh['dp'=32,'vocab'=8] {'dp','vocab'}, use_global_device_ids=true, to_apply=%region_4.5 | all-reduce | flops 2753280 | bytes 16521216 | tf_op jit(solution)/shard_map/psum | solution.py:47
  462.9 0.6 select_reduce_fusion
  464.2 1.5 dynamic_slice.5
  (6 shorter events, 0.0 us)
Async XLA Ops:
  7.2 60.5 %all-gather.5.cloned.1.call-start = ((), (), s32[]{:S(2)}) async-start(), calls=%async_computation.1 | async-start | bytes 5677056 | tf_op jit(solution)/shard_map/all_gather | solution.py:31
  7.9 117.2 %all-gather.3.cloned.1.call-start = ((), (), s32[]{:S(2)}) async-start(), calls=%async_computation | async-start | bytes 7299072 | tf_op jit(solution)/shard_map/all_gather | solution.py:35
  217.3 76.6 %copy-start = (f32[768,512]{0,1:T(8,128)S(1)}, f32[768,512]{0,1:T(8,128)}, u32[]{:S(2)}) copy-start(f32[768,512]{0,1:T(8,128)} %get-tuple-element.22) | copy-start | bytes 4718596
  293.9 8.7 %slice-start = ((s8[5505024]{0:T(1024)(128)(4,1)}), s8[4194304]{0:T(1024)(128)(4,1)S(1)}, s32[]{:S(2)}) async-start(s8[5505024]{0:T(1024)(128)(4,1)} %bitcast.13), calls=%async_computation.2 | async-start | bytes 8388608
  294.4 8.2 %slice-start.1 = ((s8[5505024]{0:T(1024)(128)(4,1)}), s8[1310720]{0:T(1024)(128)(4,1)S(1)}, s32[]{:S(2)}) async-start(s8[5505024]{0:T(1024)(128)(4,1)} %bitcast.13), calls=%async_computation.3 | async-start | bytes 2621440
Sparse Core Ops, SparseCore 0:
  10.5 57.1 all-gather.4
  70.2 54.7 all-gather.2
where the time goes:
time: 474 us
  blocking collectives  315 us (66%)
  waiting for transfers between devices  89.3 us (19%)
  matrix products  29.9 us (6%)
  local copies, waits for them, and re-layouts  18.2 us (4%)
  between operations  17.9 us (4%)
    psum x2, blocking collectives, per_device(): lax.psum((jnp.sum(teacher_weights, axis=1), jnp.sum(jnp.exp(student_logit...  224 us
    pmax x1, blocking collectives, per_device(): lax.pmax((jnp.max(teacher_logits, axis=1), jnp.max(student_logits, axis=1...  75.6 us
    all_gather x1, waiting for transfers between devices, per_device(): lax.all_gather(teacher_hidden, 'dp', axis=0, tiled=True)  49.5 us
    all_gather x1, waiting for transfers between devices, per_device(): gathered = lax.all_gather(student_hidden, 'dp', axis=0, tiled=True)  38.4 us
    unnamed x1, blocking collectives  14.7 us
    unnamed x14, local copies, waits for them, and re-layouts  9.54 us
  transfers between devices with their start and end apart: 2, of which 2 were waited for; matrix products, arithmetic and copies ran while one was open for 2% of the time, Pallas kernels for 0%

commit v1 on v0

--- a/solution.py
+++ b/solution.py
@@ -45,12 +45,15 @@
     )
     teacher_weights = jnp.exp(teacher_logits - teacher_top[:, None])
     teacher_sum, student_sum, cross_sum = lax.psum(
-        (
-            jnp.sum(teacher_weights, axis=1),
-            jnp.sum(jnp.exp(student_logits - student_top[:, None]), axis=1),
-            jnp.sum(teacher_weights * (teacher_logits - student_logits), axis=1),
+        lax.psum(
+            (
+                jnp.sum(teacher_weights, axis=1),
+                jnp.sum(jnp.exp(student_logits - student_top[:, None]), axis=1),
+                jnp.sum(teacher_weights * (teacher_logits - student_logits), axis=1),
+            ),
+            "vocab",
         ),
-        ("dp", "vocab"),
+        "dp",
     )
     teacher_norm = teacher_top + jnp.log(teacher_sum)
     student_norm = student_top + jnp.log(student_sum)

time: 474 us -> 547 us (1.15)
  blocking collectives: 315 us -> 389 us
    psum x0 -> x2, blocking collectives: none -> 277 us  [the longest x1 151 us: per_device(): lax.psum(lax.dot_general(logit_grad, student_head, (((1,), (1,)), ((), ()...]
    psum x2 -> x1, blocking collectives: 224 us -> 22 us  [per_device(): lax.psum((jnp.sum(teacher_weights, axis=1), jnp.sum(jnp.exp(student_logit...]
where the time goes in v1:
time: 547 us
  blocking collectives  389 us (71%)
  waiting for transfers between devices  89.3 us (16%)
  matrix products  27.5 us (5%)
  local copies, waits for them, and re-layouts  19.2 us (4%)
  between operations  17.8 us (3%)
    psum x1, blocking collectives, per_device(): lax.psum(lax.dot_general(logit_grad, student_head, (((1,), (1,)), ((), ()...  151 us
    psum x1, blocking collectives, per_device(): lax.psum(lax.psum((jnp.sum(teacher_weights, axis=1), jnp.sum(jnp.exp(stud...  126 us
    pmax x1, blocking collectives, per_device(): lax.pmax((jnp.max(teacher_logits, axis=1), jnp.max(student_logits, axis=1...  75.6 us
    all_gather x1, waiting for transfers between devices, per_device(): lax.all_gather(teacher_hidden, 'dp', axis=0, tiled=True)  49.5 us
    all_gather x1, waiting for transfers between devices, per_device(): gathered = lax.all_gather(student_hidden, 'dp', axis=0, tiled=True)  38.4 us
    psum x1, blocking collectives, per_device(): lax.psum((jnp.sum(teacher_weights, axis=1), jnp.sum(jnp.exp(student_logit...  22 us
    unnamed x1, blocking collectives  14.7 us
  transfers between devices with their start and end apart: 2, of which 2 were waited for; matrix products, arithmetic and copies ran while one was open for 2% of the time, Pallas kernels for 0%

profile of v1, /device:TPU:1, one launch (start us, length us, event | category | flops | bytes accessed | tf_op | source)
XLA Modules:
  0.0 546.6 jit_solution(4546018690809414506)
XLA Ops:
  7.2 0.0 all-gather.5.cloned.1.call-start
  7.2 0.7 all-gather.5.cloned.1.call-update
  7.9 0.0 all-gather.3.cloned.1.call-start
  7.9 0.7 all-gather.3.cloned.1.call-update
  9.9 1.3 dynamic-slice
  11.9 0.8 dynamic-update-slice
  12.6 0.8 dynamic-update-slice.1
  13.4 0.8 dynamic-update-slice.2
  14.2 14.7 %all-reduce.3 = (s32[32]{0:T(128)S(1)}, s32[32]{0:T(128)S(1)}, s32[768]{0:T(1024)S(1)}) all-reduce(s32[32]{0:T(128)S(1)} %dynamic-update-slice, s32[32]{0:T(128)S(1)} %dynamic-update-slice.1, s32[768]{0:T(1024)S(1)} %dynamic-update-slice.2), channel_id=1, replica_groups=mesh['dp'=32,'vocab'=8] {'dp'}, use_global_device_ids=true, to_apply=%add | all-reduce | flops 832 | bytes 6656
  28.9 0.1 iota_compare_fusion.1
  29.0 0.1 lt.42
  29.1 0.1 iota_compare_fusion
  29.2 0.1 lt.45
  29.3 38.4 %all-gather.5.cloned.1.call-done = bf16[768,3584]{1,0:T(8,128)(2,1)} async-done(((bf16[24,3584]{1,0:T(8,128)(2,1)}), bf16[768,3584]{1,0:T(8,128)(2,1)}) %all-gather.5.cloned.1.call-update) | async-done | bytes 5505040 | tf_op jit(solution)/shard_map/all_gather | solution.py:31
  67.7 7.9 %fusion.4 = (f32[768]{0:T(1024)S(1)}, f32[768,512]{0,1:T(8,128)}) fusion(bf16[768,3584]{1,0:T(8,128)(2,1)} %all-gather.5.cloned.1.call-done, bf16[3584,512]{1,0:T(8,128)(2,1)} %param.9), kind=kOutput, calls=%fused_computation.17 | convolution fusion | flops 2818964736 | bytes 10750976 | tf_op jit(solution)/shard_map/dot_general | solution.py:33
  75.6 49.5 %all-gather.3.cloned.1.call-done = bf16[768,4608]{1,0:T(8,128)(2,1)} async-done(((bf16[24,4608]{1,0:T(8,128)(2,1)}), bf16[768,4608]{1,0:T(8,128)(2,1)}) %all-gather.3.cloned.1.call-update) | async-done | bytes 7077904 | tf_op jit(solution)/shard_map/all_gather | solution.py:35
  125.1 9.3 %fusion.5 = f32[768,512]{1,0:T(8,128)} fusion(bf16[768,4608]{1,0:T(8,128)(2,1)} %all-gather.3.cloned.1.call-done, bf16[4608,512]{1,0:T(8,128)(2,1)} %param.10), kind=kOutput, calls=%fused_computation.18 | convolution fusion | flops 3623878656 | bytes 13369344 | tf_op jit(solution)/shard_map/dot_general | solution.py:34
  134.4 6.6 %scatter_custom_fusion = f32[768,512]{1,0:T(8,128)S(1)} fusion(s32[768]{0:T(1024)S(1)} %compare_select_fusion, f32[768,512]{1,0:T(8,128)} %fusion.5, f32[]{:T(128)} %constant.12.clone.1), kind=kCustom, calls=%fused_computation.8 | custom fusion | bytes 1573376 | tf_op jit(solution)/shard_map/scatter | solution.py:41
  140.9 0.5 copy.12
  141.4 0.2 reduce_max.18
  141.6 75.6 %all-reduce.4 = (f32[768]{0:T(1024)S(1)}, f32[768]{0:T(1024)S(1)}) all-reduce(f32[768]{0:T(1024)S(1)} %get-tuple-element.26, f32[768]{0:T(1024)S(1)} %reduce_max.18), channel_id=1, replica_groups=mesh['dp'=32,'vocab'=8] {'dp','vocab'}, use_global_device_ids=true, to_apply=%region_10.11 | all-reduce | flops 1536 | bytes 12288 | tf_op jit(solution)/shard_map/pmax | solution.py:43
  217.2 0.0 copy-start
  217.2 2.1 multiply_reduce_fusion
  219.3 22.0 %all-reduce.6 = (f32[768]{0:T(1024)S(1)}, f32[768]{0:T(1024)S(1)}, f32[768]{0:T(1024)S(1)}) all-reduce(f32[768]{0:T(1024)S(1)} %get-tuple-element.11, f32[768]{0:T(1024)S(1)} %get-tuple-element.10, f32[768]{0:T(1024)S(1)} %get-tuple-element.9), channel_id=1, replica_groups=mesh['dp'=32,'vocab'=8] {'vocab'}, use_global_device_ids=true, to_apply=%region_12.13 | all-reduce | flops 2304 | bytes 18432 | tf_op jit(solution)/shard_map/psum | solution.py:48
  241.3 126.0 %all-reduce.5 = (f32[768]{0:T(1024)S(1)}, f32[768]{0:T(1024)S(1)}, f32[768]{0:T(1024)S(1)}) all-reduce(f32[768]{0:T(1024)S(1)} %get-tuple-element.20, f32[768]{0:T(1024)S(1)} %get-tuple-element.21, f32[768]{0:T(1024)S(1)} %get-tuple-element.22), channel_id=1, replica_groups=mesh['dp'=32,'vocab'=8] {'dp'}, use_global_device_ids=true, to_apply=%region_13.14 | all-reduce | flops 2304 | bytes 18432 | tf_op jit(solution)/shard_map/psum | solution.py:47
  367.3 0.0 copy-start.1
  367.3 0.6 select_reduce_fusion
  367.9 0.0 copy-done
  367.9 0.0 slice-start
  367.9 0.5 select_convert_fusion
  368.4 0.9 copy-done.1
  369.4 0.0 slice-start.1
  369.4 5.8 %fusion.6 = f32[768,3584]{1,0:T(8,128)} fusion(bf16[768,512]{0,1:T(8,128)(2,1)S(1)} %select_convert_fusion, bf16[3584,512]{1,0:T(8,128)(2,1)S(1)} %copy-done.1), kind=kOutput, calls=%fused_computation.19 | convolution fusion | flops 2818572288 | bytes 15466496 | tf_op jit(solution)/shard_map/dot_general | solution.py:71
  375.1 0.0 slice-done
  375.1 0.0 slice-done.1
  375.1 4.5 fusion
  379.6 5.9 %copy.15 = bf16[3584,512]{1,0:T(8,128)(2,1)} copy(bf16[3584,512]{0,1:T(8,128)(2,1)} %fusion) | data formatting | bytes 7340032
  385.6 151.0 %all-reduce.8 = bf16[768,3584]{1,0:T(8,128)(2,1)} all-reduce(f32[768,3584]{1,0:T(8,128)} %fusion.6), channel_id=1, replica_groups=mesh['dp'=32,'vocab'=8] {'dp','vocab'}, use_global_device_ids=true, to_apply=%region_15.16 | all-reduce | flops 2752512 | bytes 16515072 | tf_op jit(solution)/shard_map/psum | solution.py:70
  537.2 1.5 dynamic_slice.5
  (5 shorter events, 0.0 us)
Async XLA Ops:
  7.2 60.5 %all-gather.5.cloned.1.call-start = ((), (), s32[]{:S(2)}) async-start(), calls=%async_computation.1 | async-start | bytes 5677056 | tf_op jit(solution)/shard_map/all_gather | solution.py:31
  7.9 117.2 %all-gather.3.cloned.1.call-start = ((), (), s32[]{:S(2)}) async-start(), calls=%async_computation | async-start | bytes 7299072 | tf_op jit(solution)/shard_map/all_gather | solution.py:35
  217.2 150.7 %copy-start = (f32[768,512]{0,1:T(8,128)S(1)}, f32[768,512]{0,1:T(8,128)}, u32[]{:S(2)}) copy-start(f32[768,512]{0,1:T(8,128)} %get-tuple-element.27) | copy-start | bytes 4718596
  367.3 2.0 copy-start.1
  367.9 7.2 %slice-start = ((s8[5505024]{0:T(1024)(128)(4,1)}), s8[4194304]{0:T(1024)(128)(4,1)S(1)}, s32[]{:S(2)}) async-start(s8[5505024]{0:T(1024)(128)(4,1)} %bitcast.13), calls=%async_computation.2 | async-start | bytes 8388608
  369.4 5.8 %slice-start.1 = ((s8[5505024]{0:T(1024)(128)(4,1)}), s8[1310720]{0:T(1024)(128)(4,1)S(1)}, s32[]{:S(2)}) async-start(s8[5505024]{0:T(1024)(128)(4,1)} %bitcast.13), calls=%async_computation.3 | async-start | bytes 2621440
Sparse Core Ops, SparseCore 0:
  10.5 57.1 all-gather.4
  70.2 54.7 all-gather.2
